TPU v7x, 256 devices: a whole 4x4x8 slice. The times are simulated.
256 devices in a mesh: row: 8 (over z), col: 8 (over x, core), rep: 4 (over y).
Axes of the slice: x: 4, y: 4, z: 8, core: 2. Of those that a mesh axis runs over, the one named last changes fastest.
Arguments:
- tensor_tiles: bfloat16 [1024, 4, 128, 128], P(('row', 'col', 'rep')), may hold values from -12 to 12
- tile_pairs: int32 [1024], P(('row', 'col', 'rep')), may hold values from 0 to 3, as said below
- tile_counts: int32 [256], P(('row', 'col', 'rep')), may hold values from 1 to 4, as said below
- occupied: bfloat16 [4096, 4096], P(('col', 'rep'), 'row'), as said below
- virtual: bfloat16 [4096, 4096], P(('col', 'rep'), 'row'), as said below
Outputs:
- polar: float32 [4, 4], replicated
- dressed: bfloat16 [4096, 4, 4096], P(('col', 'rep'), None, 'row')
Inputs may be any that keep to these rules, and one draw needn't show every extreme that they name: `tile_pairs`: the 4 entries of one block are distinct: a permutation of its tile pairs. `tile_counts`: some block has all 4 entries live. `occupied`: Symmetric. `virtual`: Symmetric.
All inputs are finite; a program needn't handle non-finite values.
Results may differ from a plain program's by a relative error of at most 0.0049.
Values may be sent and summed in bfloat16 or wider, within the bound.
A program may use at most 128 MiB of HBM per device.

v0:
```python
import jax
import jax.numpy as jnp
from jax import lax
from jax.sharding import PartitionSpec as P


def on_device(tensor_tiles, tile_pairs, tile_counts, occupied, virtual):
    tile_size = tensor_tiles.shape[-1]
    aux_count = tensor_tiles.shape[1]
    owned = tile_counts[0]
    panel = lax.all_gather(virtual, ("col", "rep"), axis=0, tiled=True)
    occupied_block = lax.all_gather(occupied, "row", axis=1, tiled=True)
    total_ao = panel.shape[0]
    sigma_width = panel.shape[1]
    mu_width = occupied.shape[0]
    nu_tiles = sigma_width // tile_size

    def place(buffer, contrib):
        return buffer + contrib

    def visit(index, buffer):
        pair = tile_pairs[index]
        block = lax.dynamic_slice(
            panel, (0, pair % nu_tiles * tile_size), (sigma_width * lax.axis_size("row"), tile_size)
        )
        contrib = jnp.einsum(
            "sn,pmn->spm", block, tensor_tiles[index], preferred_element_type=jnp.float32
        )
        return place(buffer, contrib)

    start_buffer = jnp.zeros((sigma_width * lax.axis_size("row"), aux_count, mu_width), jnp.float32)
    mixed = lax.psum_scatter(
        lax.fori_loop(0, owned, visit, start_buffer), "row", scatter_dimension=0, tiled=True
    )
    half_product = mixed.astype(jnp.bfloat16)
    block = occupied_block
    dressed_sum = lax.psum_scatter(
        jnp.einsum("ml,spm->lps", block, half_product, preferred_element_type=jnp.float32),
        ("col", "rep"),
        scatter_dimension=0,
        tiled=True,
    )
    dressed = dressed_sum.astype(jnp.bfloat16)

    def pairing(index, running):
        pair = tile_pairs[index]
        corner = (pair // nu_tiles * tile_size, 0, pair % nu_tiles * tile_size)
        region = lax.dynamic_slice(dressed, corner, (tile_size, aux_count, tile_size))
        return running + jnp.einsum(
            "pls,lqs->pq", tensor_tiles[index], region, preferred_element_type=jnp.float32
        )

    own_share = lax.fori_loop(0, owned, pairing, jnp.zeros((aux_count, aux_count), jnp.float32))
    polar = lax.psum(own_share, ("row", "col", "rep")) / total_ao
    return (polar, dressed)


def solution(mesh):
    return jax.shard_map(
        on_device,
        mesh=mesh,
        in_specs=(
            P(("row", "col", "rep"), None, None, None),
            P(("row", "col", "rep")),
            P(("row", "col", "rep")),
            P(("col", "rep"), "row"),
            P(("col", "rep"), "row"),
        ),
        out_specs=(P(), P(("col", "rep"), None, "row")),
        check_vma=False,
    )
```

profile of v0, /device:TPU:1, one launch (start us, length us, event | category | flops | bytes accessed | tf_op | source)
XLA Modules:
  0.0 497.3 jit_solution(6712619987267052564)
XLA Ops:
  7.2 0.0 copy-start.2
  7.2 0.0 copy-start
  7.2 0.0 all-gather.3.cloned.1.call-start
  7.2 0.7 all-gather.3.cloned.1.call-update
  7.9 0.0 all-gather.5.cloned.1.call-start
  8.0 0.7 all-gather.5.cloned.1.call-update
  8.7 0.0 reduce-scatter.3.cloned.1.call-start
  8.7 57.2 %all-gather.3.cloned.1.call-done = bf16[4096,512]{1,0:T(8,128)(2,1)} async-done(((bf16[128,512]{1,0:T(8,128)(2,1)}), bf16[4096,512]{1,0:T(8,128)(2,1)}) %all-gather.3.cloned.1.call-update) | async-done | bytes 4194320 | tf_op jit(solution)/shard_map/all_gather | solution.py:11
  65.9 3.8 broadcast_in_dim.3
  69.7 0.0 copy-done.2
  69.7 0.0 copy-done
  69.7 46.5 %while.24 = (s32[]{:T(128)}, f32[4096,4,128]{2,0,1:T(8,128)}, s32[]{:T(128)}, s32[4]{0:T(128)S(1)}, bf16[4096,512]{1,0:T(8,128)(2,1)}, /*index=5*/bf16[4,4,128,1...) while((s32[]{:T(128)}, f32[4096,4,128]{2,0,1:T(8,128)}, ...), condition=%wide.region_1.2_spmd, body=%wide.region_0.1_spmd.sunk | while | flops 538968064 | bytes 17957188 | solution.py:33
  70.4 0.6 dynamic_slice.56
  72.9 8.2 %convolution_add_fusion.2 = f32[4096,4,128]{2,0,1:T(8,128)} fusion(f32[4096,4,128]{2,0,1:T(8,128)} %get-tuple-element.287, bf16[4096,512]{1,0:T(8,128)(2,1)} %get-tuple-element.302, s32[]{:T(128)S(6)} %select_n.58, bf16[4,4,128,128]{3,2,1,0:T(8,128)(2,1)S(1)} %get-tuple-element.303, s32[]{:T(128)S(6)} %select_n.56), kind=kOutput, calls=%fused_computation.clone.1 | convolution fusion | flops 538968064 | bytes 17956872 | tf_op jit(solution)/shard_map/while/body/sn,pmn->spm/dot_general | solution.py:26
  81.8 0.6 dynamic_slice.56
  84.3 8.3 %convolution_add_fusion.2 = f32[4096,4,128]{2,0,1:T(8,128)} fusion(f32[4096,4,128]{2,0,1:T(8,128)} %get-tuple-element.287, bf16[4096,512]{1,0:T(8,128)(2,1)} %get-tuple-element.302, s32[]{:T(128)S(6)} %select_n.58, bf16[4,4,128,128]{3,2,1,0:T(8,128)(2,1)S(1)} %get-tuple-element.303, s32[]{:T(128)S(6)} %select_n.56), kind=kOutput, calls=%fused_computation.clone.1 | convolution fusion | flops 538968064 | bytes 17956872 | tf_op jit(solution)/shard_map/while/body/sn,pmn->spm/dot_general | solution.py:26
  93.3 0.6 dynamic_slice.56
  95.8 8.3 %convolution_add_fusion.2 = f32[4096,4,128]{2,0,1:T(8,128)} fusion(f32[4096,4,128]{2,0,1:T(8,128)} %get-tuple-element.287, bf16[4096,512]{1,0:T(8,128)(2,1)} %get-tuple-element.302, s32[]{:T(128)S(6)} %select_n.58, bf16[4,4,128,128]{3,2,1,0:T(8,128)(2,1)S(1)} %get-tuple-element.303, s32[]{:T(128)S(6)} %select_n.56), kind=kOutput, calls=%fused_computation.clone.1 | convolution fusion | flops 538968064 | bytes 17956872 | tf_op jit(solution)/shard_map/while/body/sn,pmn->spm/dot_general | solution.py:26
  104.8 0.6 dynamic_slice.56
  107.3 8.2 %convolution_add_fusion.2 = f32[4096,4,128]{2,0,1:T(8,128)} fusion(f32[4096,4,128]{2,0,1:T(8,128)} %get-tuple-element.287, bf16[4096,512]{1,0:T(8,128)(2,1)} %get-tuple-element.302, s32[]{:T(128)S(6)} %select_n.58, bf16[4,4,128,128]{3,2,1,0:T(8,128)(2,1)S(1)} %get-tuple-element.303, s32[]{:T(128)S(6)} %select_n.56), kind=kOutput, calls=%fused_computation.clone.1 | convolution fusion | flops 538968064 | bytes 17956872 | tf_op jit(solution)/shard_map/while/body/sn,pmn->spm/dot_general | solution.py:26
  116.2 0.0 reduce-scatter.3.cloned.1.call-update
  116.2 0.0 reduce-scatter.5.cloned.1.call-start
  116.3 0.0 all-gather.5.cloned.1.call-done
  116.3 93.9 %reduce-scatter.3.cloned.1.call-done = f32[512,4,128]{2,0,1:T(8,128)} async-done(((f32[4096,4,128]{2,0,1:T(8,128)}), f32[512,4,128]{2,0,1:T(8,128)}) %reduce-scatter.3.cloned.1.call-update) | async-done | bytes 1048592 | tf_op jit(solution)/shard_map/reduce_scatter | solution.py:32
  210.3 17.1 %convolution_bitcast_fusion.1 = f32[4096,4,512]{0,2,1:T(8,128)} fusion(bf16[128,4096]{1,0:T(8,128)(2,1)} %all-gather.5.cloned.1.call-done, f32[512,4,128]{2,0,1:T(8,128)} %reduce-scatter.3.cloned.1.call-done), kind=kOutput, calls=%fused_computation.12 | convolution fusion | flops 2147745792 | bytes 35651584 | tf_op jit(solution)/shard_map/ml,spm->lps/dot_general | solution.py:38
  227.4 0.0 reduce-scatter.5.cloned.1.call-update
  227.4 170.9 %reduce-scatter.5.cloned.1.call-done = f32[128,4,512]{0,2,1:T(8,128)} async-done(((f32[4096,4,512]{0,2,1:T(8,128)}), f32[128,4,512]{0,2,1:T(8,128)}) %reduce-scatter.5.cloned.1.call-update) | async-done | bytes 1048592 | tf_op jit(solution)/shard_map/reduce_scatter | solution.py:37
  398.3 1.3 convert_element_type.7
  399.6 0.4 copy.8
  400.0 14.8 %while.25 = (s32[]{:T(128)}, f32[4,4]{1,0:T(4,128)S(1)}, s32[]{:T(128)}, bf16[4,4,128,128]{3,2,1,0:T(8,128)(2,1)S(1)}, s32[4]{0:T(128)S(1)}, /*index=5*/bf16[128...) while((s32[]{:T(128)}, f32[4,4]{1,0:T(4,128)S(1)}, ...), condition=%wide.region_5.6_spmd, body=%wide.region_4.5_spmd.sunk | while | flops 524324 | bytes 526726 | solution.py:53
  400.7 0.6 dynamic_slice.59
  403.2 0.3 fusion.17
  404.2 0.6 dynamic_slice.59
  406.8 0.3 fusion.17
  407.7 0.6 dynamic_slice.59
  410.3 0.3 fusion.17
  411.3 0.6 dynamic_slice.59
  413.8 0.3 fusion.17
  414.8 0.0 copy-start.1
  414.8 75.4 %psum.7 = f32[4,4]{1,0:T(4,128)S(1)} all-reduce(f32[4,4]{1,0:T(4,128)S(1)} %get-tuple-element.165), channel_id=1, replica_groups=mesh['row'=8,'col'=8,'rep'=4] {'row','col','rep'}, use_global_device_ids=true, to_apply=%region_6.7 | all-reduce | flops 16 | bytes 128 | tf_op jit(solution)/shard_map/psum | solution.py:54
  490.1 0.6 broadcast_multiply_fusion
  490.7 0.0 copy-done.1
  (5 shorter events, 0.1 us)
Async XLA Ops:
  7.2 62.5 %copy-start.2 = (s32[4]{0:T(128)S(1)}, s32[4]{0:T(128)}, u32[]{:S(2)}) copy-start(s32[4]{0:T(128)} %param.10) | copy-start | bytes 52
  7.2 62.5 %copy-start = (bf16[4,4,128,128]{3,2,1,0:T(8,128)(2,1)S(1)}, bf16[4,4,128,128]{3,2,1,0:T(8,128)(2,1)}, u32[]{:S(2)}) copy-start(bf16[4,4,128,128]{3,2,1,0:T(8,128)(2,1)} %param.9) | copy-start | bytes 1572868
  7.2 58.7 %all-gather.3.cloned.1.call-start = ((), (), s32[]{:S(2)}) async-start(), calls=%async_computation.2 | async-start | bytes 4325376 | tf_op jit(solution)/shard_map/all_gather | solution.py:11
  7.9 108.4 %all-gather.5.cloned.1.call-start = ((), (), s32[]{:S(2)}) async-start(), calls=%async_computation.4 | async-start | bytes 1179648 | tf_op jit(solution)/shard_map/all_gather | solution.py:12
  8.7 201.6 %reduce-scatter.3.cloned.1.call-start = ((), (), s32[]{:S(2)}) async-start(), calls=%async_computation.3 | async-start | bytes 9437184 | tf_op jit(solution)/shard_map/reduce_scatter | solution.py:32
  116.2 282.1 %reduce-scatter.5.cloned.1.call-start = ((), (), s32[]{:S(2)}) async-start(), calls=%async_computation.5 | async-start | bytes 34603008 | tf_op jit(solution)/shard_map/reduce_scatter | solution.py:37
  414.8 76.0 %copy-start.1 = (bf16[128,4,512]{2,1,0:T(4,128)(2,1)}, bf16[128,4,512]{2,1,0:T(4,128)(2,1)S(1)}, u32[]{:S(2)}) copy-start(bf16[128,4,512]{2,1,0:T(4,128)(2,1)S(1)} %get-tuple-element.359) | copy-start | bytes 1572868
Sparse Core Ops, SparseCore 0:
  10.6 55.2 all-gather.2
  67.7 32.6 all-gather.4
  116.4 93.8 reduce-scatter.2
  227.5 170.7 reduce-scatter.4
where the time goes:
time: 497 us
  waiting for transfers between devices  323 us (65%)
  blocking collectives  75.4 us (15%)
  matrix products  51.2 us (10%)
  loops' own time  22.4 us (5%)
  between operations  13.8 us (3%)
  local copies, waits for them, and re-layouts  8.95 us (2%)
    reduce_scatter x1, waiting for transfers between devices, on_device(): lax.psum_scatter(jnp.einsum('ml,spm->lps', block, half_product, preferred...  171 us
    reduce_scatter x1, waiting for transfers between devices, on_device(): lax.psum_scatter(lax.fori_loop(0, owned, visit, start_buffer), 'row', sca...  93.9 us
    psum x1, blocking collectives, on_device(): polar = lax.psum(own_share, ('row', 'col', 'rep')) / total_ao  75.4 us
    all_gather x1, waiting for transfers between devices, on_device(): panel = lax.all_gather(virtual, ('col', 'rep'), axis=0, tiled=True)  57.2 us
    dot_general x4, matrix products, visit(): jnp.einsum('sn,pmn->spm', block, tensor_tiles[index], preferred_element_t...  33 us
    dot_general x1, matrix products, on_device(): jnp.einsum('ml,spm->lps', block, half_product, preferred_element_type=jnp...  17.1 us
    another operation x1, loops' own time, on_device(): lax.fori_loop(0, owned, pairing, jnp.zeros((aux_count, aux_count), jnp.fl...  11.2 us
    another operation x1, loops' own time, on_device(): lax.fori_loop(0, owned, visit, start_buffer)  11.2 us
  transfers between devices with their start and end apart: 4, of which 3 were waited for; matrix products, arithmetic and copies ran while one was open for 8% of the time, Pallas kernels for 0%

commit v1 on v0

v1 whole, which is shorter than its diff:
```python
import jax
import jax.numpy as jnp
from jax import lax
from jax.experimental import pallas as pl
from jax.experimental.pallas import tpu as pltpu
from jax.sharding import PartitionSpec as P

MESH = pl.DeviceIdType.MESH
F32, BF16 = jnp.float32, jnp.bfloat16
TILE, WIDTH, AUX = 128, 512, 4
NZ, NX, NY = 8, 4, 4
HALF = TILE // 2
OCC = 4


def kernel(
    tiles, pairs, counts, occ, virt, polar, dressed,
    bl, zb, vp, ob, hg, ps, pr, pf, qs, qa, qb,
    zs, zr, vs, vr, us, ur, os_, or_, ys, yr, ks, kr, xs, xr, qss, qsr,
):
    z, col, y = lax.axis_index("row"), lax.axis_index("col"), lax.axis_index("rep")
    x, core = col // 2, col % 2
    sent = []

    def at_z(d):
        return ((z + d) % NZ, col, y)

    def at_x(d):
        return (z, (col + 2 * d) % (2 * NX), y)

    def at_y(d):
        return (z, col, (y + d) % NY)

    def at_xy(dx, dy):
        return (z, (col + 2 * dx) % (2 * NX), (y + dy) % NY)

    sibling = (z, x * 2 + 1 - core, y)

    def remote(src, dst, send, recv, to):
        return pltpu.make_async_remote_copy(
            src_ref=src, dst_ref=dst, send_sem=send, recv_sem=recv, device_id=to, device_id_type=MESH
        )

    def go(copy):
        copy.start()
        sent.append(copy)

    barrier = pltpu.get_barrier_semaphore()
    partners = [at_z(d) for d in range(1, NZ)]
    partners += [at_xy(dx, dy) for dx in range(NX) for dy in range(NY) if dx or dy]
    partners += [sibling]
    for to in partners:
        pl.semaphore_signal(barrier, inc=1, device_id=to, device_id_type=MESH)

    live = counts[0]
    for q in range(4):
        where = jnp.int32(0)
        for t in range(1, 4):
            where = jnp.where(pairs[t] == q, jnp.int32(t), where)
        keep = where < live
        for p in range(AUX):
            tile = tiles[where, p]
            tile = jnp.where(keep, tile, jnp.zeros_like(tile))
            bl[p, :, q * TILE : (q + 1) * TILE] = tile
    zb[OCC, 0] = occ[...]
    for p in range(AUX):
        zb[p, 0] = bl[p]
    vp[x, core, y] = virt[...]

    pl.semaphore_wait(barrier, len(partners))

    def ring(a, k, way, sub):
        slot_from = (NZ - (k - 1)) % NZ if way == 0 else k - 1
        slot_to = NZ - k if way == 0 else k
        rows = pl.ds(sub * HALF, HALF)
        return remote(
            zb.at[a, slot_from, rows], zb.at[a, slot_to, rows],
            zs.at[a, k - 1, way, sub], zr.at[a, k - 1, way, sub], at_z(1 if way == 0 else -1),
        )

    def legs(k):
        if k == 4:
            return [(0, 0), (1, 1)]
        return [(0, 0), (1, 0), (0, 1), (1, 1)]

    def z_start(a):
        for way, sub in legs(1):
            go(ring(a, 1, way, sub))

    def z_step(a, k):
        for way, sub in legs(k):
            ring(a, k, way, sub).wait_recv()
            if k < 4 and (way, sub) in legs(k + 1):
                go(ring(a, k + 1, way, sub))

    def v_block(j):
        return (
            jnp.where(core == 0, x, (x - j + NX) % NX),
            jnp.where(core == 0, (y - j + NY) % NY, y),
        )

    def v_peer(d, first):
        on_y = jnp.where(core == 0, 1, 0) if first else jnp.where(core == 0, 0, 1)
        dx, dy = d * (1 - on_y), d * on_y
        return (z, (col + 2 * dx) % (2 * NX), (y + dy) % NY)

    def v_copy(j, d, first):
        bx, by = v_block(j)
        i = d - 1 if first else 3 + j * 3 + d - 1
        ref = vp.at[bx, core, by]
        return remote(ref, ref, vs.at[i], vr.at[i], v_peer(d, first))

    def v_landed(j, d):
        bx, by = v_block(j)
        bx = jnp.where(core == 0, (x - d + NX) % NX, bx)
        by = jnp.where(core == 0, by, (y - d + NY) % NY)
        return bx, by

    def v_swap(j, d):
        bx, by = v_landed(j, d)
        ref = vp.at[bx, core, by]
        return remote(ref, ref, us.at[j, d], ur.at[j, d], sibling)

    def v_start():
        for d in (1, 3, 2):
            go(v_copy(0, d, True))
        for d in (1, 3, 2):
            go(v_copy(0, d, False))
        go(v_swap(0, 0))

    def v_first(j):
        v_copy(0, j, True).wait_recv()
        for d in (1, 3, 2):
            go(v_copy(j, d, False))
        go(v_swap(j, 0))

    def v_second(j):
        for d in (1, 3, 2):
            v_copy(j, d, False).wait_recv()
            go(v_swap(j, d))

    def v_done():
        for j in range(4):
            for d in range(4):
                v_swap(j, d).wait_recv()

    def z_dots(a, offsets, total=None):
        for s in offsets:
            m = (z + s) % NZ
            v = vp[m // 2, m % 2].reshape(WIDTH, WIDTH)
            term = jnp.dot(zb[a, s], v, preferred_element_type=F32)
            total = term if total is None else total + term
        return total

    def o_copy(d, h):
        m = 2 * ((x + d) % NX) + h
        slot = (m - z + NZ) % NZ
        return remote(
            zb.at[OCC, slot], ob.at[h, NX - d], os_.at[d - 1, h], or_.at[d - 1, h], at_x(d)
        )

    def o_start():
        for d in (2, 1, 3):
            for h in range(2):
                go(o_copy(d, h))
        for h in range(2):
            ob[h, 0] = zb[OCC, (2 * x + h - z + NZ) % NZ]

    def o_done():
        for d in (2, 1, 3):
            for h in range(2):
                o_copy(d, h).wait_recv()

    def y_copy(p, d):
        ref = hg.at[p, core, y]
        return remote(ref, ref, ys.at[p, d - 1], yr.at[p, d - 1], at_y(d))

    def y_swap(p, j):
        ref = hg.at[p, core, (y - j + NY) % NY]
        return remote(ref, ref, ks.at[p, j], kr.at[p, j], sibling)

    def y_start(p, value):
        hg[p, core, y] = value
        for d in (2, 1, 3):
            go(y_copy(p, d))
        go(y_swap(p, 0))

    def y_done(p):
        for d in (1, 3, 2):
            y_copy(p, d).wait_recv()
            go(y_swap(p, d))

    def x_copy(p, d):
        return remote(ps.at[p, d - 1], pr.at[p, d - 1], xs.at[p, d - 1], xr.at[p, d - 1], at_x(d))

    def x_start(p):
        for j in range(4):
            y_swap(p, j).wait_recv()
        h0 = hg[p, 0].reshape(WIDTH, WIDTH)
        h1 = hg[p, 1].reshape(WIDTH, WIDTH)
        for d in (2, 1, 3):
            part = jnp.dot(ob[0, d], h0, preferred_element_type=F32)
            part += jnp.dot(ob[1, d], h1, preferred_element_type=F32)
            ps[p, d - 1] = part.astype(BF16)
            go(x_copy(p, d))
        part = jnp.dot(ob[0, 0], h0, preferred_element_type=F32)
        part += jnp.dot(ob[1, 0], h1, preferred_element_type=F32)
        pf[p] = part

    def x_done(p):
        total = pf[p]
        for d in (1, 3, 2):
            x_copy(p, d).wait_recv()
            total += pr[p, d - 1].astype(F32)
        return total.astype(BF16)

    rows = lax.broadcasted_iota(jnp.int32, (8, 128), 0)
    lanes = lax.broadcasted_iota(jnp.int32, (8, 128), 1)

    def share(q, value):
        dressed[q] = value
        mine = jnp.zeros((8, 128), F32)
        d = value.astype(F32)
        for p in range(AUX):
            s = jnp.sum(bl[p].astype(F32) * d)
            mine = jnp.where((rows == p) & (lanes == q), s, mine)
        return mine

    z_start(0)
    z_start(OCC)
    v_start()
    z_step(0, 1)
    v_first(1)
    v_first(3)
    z_step(OCC, 1)
    v_first(2)
    z_step(0, 2)
    v_second(0)
    z_step(OCC, 2)
    z_step(0, 3)
    z_start(1)
    v_second(1)
    v_second(3)
    z_step(OCC, 3)
    v_second(2)
    z_step(0, 4)
    v_done()
    y_start(0, z_dots(0, range(8)).astype(BF16))
    z_step(1, 1)
    z_start(2)
    z_step(OCC, 4)
    o_start()
    z_step(1, 2)
    z_step(2, 1)
    y_done(0)
    z_step(1, 3)
    z_step(2, 2)
    o_done()
    x_start(0)
    z_step(1, 4)
    z_start(3)
    y_start(1, z_dots(1, range(8)).astype(BF16))
    z_step(2, 3)
    z_step(3, 1)
    mine = share(0, x_done(0))
    z_step(2, 4)
    y_start(2, z_dots(2, range(8)).astype(BF16))
    y_done(1)
    z_step(3, 2)
    x_start(1)
    z_step(3, 3)
    mine += share(1, x_done(1))
    y_done(2)
    x_start(2)
    last = z_dots(3, (0, 1, 2, 3, 5, 6, 7))
    z_step(3, 4)
    y_start(3, z_dots(3, (4,), last).astype(BF16))
    mine += share(2, x_done(2))
    y_done(3)
    x_start(3)
    mine += share(3, x_done(3))

    qs[0] = mine
    swap = remote(qs.at[0], qs.at[1], qss.at[0], qsr.at[0], sibling)
    go(swap)
    swap.wait_recv()
    here = x * NY + y
    qa[here] = qs[0] + qs[1]
    plane = []
    for i in range(1, NX * NY):
        ref = qa.at[here]
        plane.append(remote(ref, ref, qss.at[i], qsr.at[i], at_xy(i // NY, i % NY)))
    for copy in plane:
        go(copy)
    for copy in plane:
        copy.wait_recv()
    qb[z] = jnp.sum(qa[...], axis=0)
    line = [remote(qb.at[z], qb.at[z], qss.at[15 + d], qsr.at[15 + d], at_z(d)) for d in range(1, NZ)]
    for copy in line:
        go(copy)
    for copy in line:
        copy.wait_recv()
    polar[...] = jnp.sum(qb[...], axis=0)
    for copy in sent:
        copy.wait_send()


def on_device(tensor_tiles, tile_pairs, tile_counts, occupied, virtual):
    vmem = pl.BlockSpec(memory_space=pltpu.VMEM)
    smem = pl.BlockSpec(memory_space=pltpu.SMEM)
    dma = pltpu.SemaphoreType.DMA
    block = (TILE, WIDTH)
    shares, dressed = pl.pallas_call(
        kernel,
        out_shape=(
            jax.ShapeDtypeStruct((8, 128), F32),
            jax.ShapeDtypeStruct((AUX, *block), BF16),
        ),
        in_specs=[vmem, smem, smem, vmem, vmem],
        out_specs=(vmem, vmem),
        scratch_shapes=[
            pltpu.VMEM((AUX, *block), BF16),
            pltpu.VMEM((AUX + 1, NZ, *block), BF16),
            pltpu.VMEM((NX, 2, NY, *block), BF16),
            pltpu.VMEM((2, NX, *block), BF16),
            pltpu.VMEM((AUX, 2, NY, *block), BF16),
            pltpu.VMEM((AUX, 3, *block), BF16),
            pltpu.VMEM((AUX, 3, *block), BF16),
            pltpu.VMEM((AUX, *block), F32),
            pltpu.VMEM((2, 8, 128), F32),
            pltpu.VMEM((16, 8, 128), F32),
            pltpu.VMEM((8, 8, 128), F32),
            dma((5, 4, 2, 2)), dma((5, 4, 2, 2)),
            dma((15,)), dma((15,)),
            dma((4, 4)), dma((4, 4)),
            dma((3, 2)), dma((3, 2)),
            dma((4, 3)), dma((4, 3)),
            dma((4, 4)), dma((4, 4)),
            dma((4, 3)), dma((4, 3)),
            dma((23,)), dma((23,)),
        ],
        compiler_params=pltpu.CompilerParams(
            collective_id=0, has_side_effects=True, vmem_limit_bytes=48 * 2**20
        ),
        cost_estimate=pl.CostEstimate(flops=4 * 2**30, bytes_accessed=2**21, transcendentals=0),
    )(tensor_tiles, tile_pairs, tile_counts, occupied, virtual)
    return shares[:AUX, :AUX] / (NZ * WIDTH), dressed.transpose(1, 0, 2)


def solution(mesh):
    spread = P(("row", "col", "rep"))
    return jax.shard_map(
        on_device,
        mesh=mesh,
        in_specs=(
            P(("row", "col", "rep"), None, None, None),
            spread,
            spread,
            P(("col", "rep"), "row"),
            P(("col", "rep"), "row"),
        ),
        out_specs=(P(), P(("col", "rep"), None, "row")),
        check_vma=False,
    )
```

time: 497 us -> 109 us (0.22)
  waiting for transfers between devices: 323 us -> 0 us
  Pallas kernels: 0 us -> 103 us
  blocking collectives: 75.4 us -> 0 us
  matrix products: 51.2 us -> 0 us
  loops' own time: 22.4 us -> 0 us
  between operations: 13.8 us -> 1.32 us
    reduce_scatter x2 -> x0, waiting for transfers between devices: 265 us -> none  [the longest x1 171 us: on_device(): lax.psum_scatter(jnp.einsum('ml,spm->lps', block, half_product, preferred...]
    pallas_call x0 -> x1, Pallas kernels: none -> 103 us  [on_device(): pl.pallas_call(kernel, out_shape=(jax.ShapeDtypeStruct((8, 128), F32), ja...]
    psum x1 -> x0, blocking collectives: 75.4 us -> none  [on_device(): polar = lax.psum(own_share, ('row', 'col', 'rep')) / total_ao]
    all_gather x2 -> x0, waiting for transfers between devices: 57.2 us -> none  [the longest x1 57.2 us: on_device(): panel = lax.all_gather(virtual, ('col', 'rep'), axis=0, tiled=True)]
    dot_general x9 -> x0, matrix products: 51.2 us -> none  [the longest x4 33 us: visit(): jnp.einsum('sn,pmn->spm', block, tensor_tiles[index], preferred_element_t...]
    another operation x2 -> x0, loops' own time: 22.4 us -> none  [the longest x1 11.2 us: on_device(): lax.fori_loop(0, owned, pairing, jnp.zeros((aux_count, aux_count), jnp.fl...]
  transfers between devices with their start and end apart: 4 -> 0, of which waited for: 3 -> 0; matrix products, arithmetic and copies ran while one was open for 8% -> 0% of each run, Pallas kernels for 0% -> 0%
where the time goes in v1:
time: 109 us
  Pallas kernels  103 us (94%)
  local copies, waits for them, and re-layouts  4.05 us (4%)
  between operations  1.32 us (1%)
    pallas_call x1, Pallas kernels, on_device(): pl.pallas_call(kernel, out_shape=(jax.ShapeDtypeStruct((8, 128), F32), ja...  103 us
    unnamed x9, local copies, waits for them, and re-layouts  4.05 us

profile of v1, /device:TPU:1, one launch (start us, length us, event | category | flops | bytes accessed | tf_op | source)
XLA Modules:
  0.0 108.6 jit_solution(4442830146289585066)
XLA Ops:
  0.6 0.0 copy-start.3
  1.3 0.0 copy-done.3
  1.3 0.0 copy-start
  1.3 1.0 copy-done
  2.4 0.0 copy-start.1
  2.4 0.9 copy-done.1
  3.3 0.0 copy-start.2
  3.3 0.9 copy-done.2
  4.2 102.7 %shard_map.68 = (f32[8,128]{1,0:T(8,128)S(1)}, bf16[4,128,512]{2,1,0:T(8,128)(2,1)S(1)}) custom-call(bf16[4,4,128,128]{3,2,1,0:T(8,128)(2,1)S(1)} %copy-done, s32[4]{0:T(128)S(1)} %copy-done.3, s32[1]{0:T(128)S(6)} %copy.8.counts, bf16[128,512]{1,0:T(8,128)(2,1)S(1)} %copy-done.1, bf16[128,512]{1,0:T(8,128)(2,1)S(1)} %copy-done.2), custom_call_target="tpu_custom_call" | custom-call | flops 4294967296 | bytes 2097152 | tf_op jit(solution)/shard_map/pallas_call | solution.py:313
  106.9 0.6 slice_multiply_fusion
  107.4 1.2 %copy.7 = bf16[128,4,512]{2,1,0:T(4,128)(2,1)} copy(bf16[128,4,512]{2,0,1:T(8,128)(2,1)S(1)} %bitcast.1) | data formatting | bytes 1048576
Async XLA Ops:
  0.6 0.7 copy-start.3
  1.3 1.0 copy-start
  2.4 0.9 copy-start.1
  3.3 0.9 copy-start.2

commit v2 on v1

v2 whole, which is shorter than its diff:
```python
import jax
import jax.numpy as jnp
from jax import lax
from jax.experimental import pallas as pl
from jax.experimental.pallas import tpu as pltpu
from jax.sharding import PartitionSpec as P

MESH = pl.DeviceIdType.MESH
F32, BF16 = jnp.float32, jnp.bfloat16
TILE, WIDTH, AUX = 128, 512, 4
NZ, NX, NY = 8, 4, 4
HALF = TILE // 2
PARTS = 2
VIRT, TENSOR = 0, 1
OCC = 4


def kernel(
    tiles_in, pairs_in, counts_in, occ, virt, polar, dressed,
    tiles, pairs, counts, bl, bx, zb, vp, ob, hg, ps, pr, pf, dv, qs, qa, qb,
    zs, zr, vs, vr, us, ur, os_, or_, bs, br, ys, yr, ks, kr, xs, xr, qss, qsr, ins, outs,
):
    z, col, y = lax.axis_index("row"), lax.axis_index("col"), lax.axis_index("rep")
    x, core = col // 2, col % 2
    sent = []

    def at_z(d):
        return ((z + d) % NZ, col, y)

    def at_x(d):
        return at_xy(d, 0)

    def at_y(d):
        return at_xy(0, d)

    def at_xy(dx, dy):
        return (z, (col + 2 * dx) % (2 * NX), (y + dy) % NY)

    sibling = (z, x * 2 + 1 - core, y)

    def remote(src, dst, send, recv, to):
        return pltpu.make_async_remote_copy(
            src_ref=src, dst_ref=dst, send_sem=send, recv_sem=recv, device_id=to, device_id_type=MESH
        )

    def go(copy):
        copy.start()
        sent.append(copy)

    loads = [
        pltpu.make_async_copy(src, dst, ins.at[i])
        for i, (src, dst) in enumerate([
            (pairs_in, pairs), (counts_in, counts), (tiles_in, tiles),
            (occ, zb.at[OCC, 0]), (virt, vp.at[VIRT, x, core, y]),
        ])
    ]
    for load in loads:
        load.start()

    barrier = pltpu.get_barrier_semaphore()
    partners = [sibling] + [at_z(d) for d in range(1, NZ)]
    partners += [at_xy(dx, dy) for dx in range(NX) for dy in range(NY) if dx or dy]
    for to in partners:
        pl.semaphore_signal(barrier, inc=1, device_id=to, device_id_type=MESH)

    for load in loads:
        load.wait()

    live = counts[0]
    for q in range(4):
        where = jnp.int32(0)
        for t in range(1, 4):
            where = jnp.where(pairs[t] == q, jnp.int32(t), where)
        keep = where < live
        for p in range(AUX):
            tile = tiles[where, p]
            tile = jnp.where(keep, tile, jnp.zeros_like(tile))
            bl[p, :, q * TILE : (q + 1) * TILE] = tile
    for p in range(AUX):
        zb[p, 0] = bl[p]
    vp[TENSOR, x, core, y] = bl[AUX - 1]

    pl.semaphore_wait(barrier, len(partners))

    def ring(a, k, way, sub):
        slot_from = (NZ - (k - 1)) % NZ if way == 0 else k - 1
        slot_to = NZ - k if way == 0 else k
        rows = pl.ds(sub * (TILE // PARTS), TILE // PARTS)
        return remote(
            zb.at[a, slot_from, rows], zb.at[a, slot_to, rows],
            zs.at[a, k - 1, way, sub], zr.at[a, k - 1, way, sub], at_z(1 if way == 0 else -1),
        )

    def ways(k, sub):
        if k == 4:
            return [0] if sub < PARTS // 2 else [1]
        return [0, 1]

    def z_start(a):
        for sub in range(PARTS):
            for way in (0, 1):
                go(ring(a, 1, way, sub))

    def z_sub(a, k, sub):
        for way in (0, 1):
            ring(a, k, way, sub).wait_recv()
            if way in ways(k + 1, sub):
                go(ring(a, k + 1, way, sub))

    def z_last(a):
        for sub in range(PARTS):
            ring(a, 4, ways(4, sub)[0], sub).wait_recv()

    def block_at(j, d):
        return (x - j + NX) % NX, core, (y - d + NY) % NY

    def panel_peer(d, first):
        return at_x(d) if first else at_y(d)

    def p_send(b, j, d):
        ref = vp.at[b, *block_at(0 if j is None else j, 0)]
        i = 0 if j is None else 1 + j
        return remote(ref, ref, vs.at[b, i, 0, d // 2], vr.at[b, i, 0, d // 2], panel_peer(d, j is None))

    def p_pass(b, j, d):
        bx, bc, by = block_at(d, 0) if j is None else block_at(j, d)
        ref = vp.at[b, bx, bc, by, pl.ds(HALF * (d // 2), HALF)]
        i = 0 if j is None else 1 + j
        return remote(ref, ref, vs.at[b, i, 1, d // 2], vr.at[b, i, 1, d // 2], panel_peer(d, j is None))

    def p_swap(b, j, d):
        ref = vp.at[b, *block_at(j, d)]
        return remote(ref, ref, us.at[b, j, d], ur.at[b, j, d], sibling)

    def p_out(b, j):
        for d in (1, 3):
            go(p_send(b, j, d))
        go(p_swap(b, j, 0))

    def p_start(b):
        for d in (1, 3):
            go(p_send(b, None, d))
        p_out(b, 0)

    def p_first(b):
        for d in (1, 3):
            p_send(b, None, d).wait_recv()
            go(p_pass(b, None, d))
        for d in (1, 3):
            p_out(b, d)

    def p_first_far(b):
        for d in (1, 3):
            p_pass(b, None, d).wait_recv()
        p_out(b, 2)

    def p_second(b, j):
        for d in (1, 3):
            p_send(b, j, d).wait_recv()
            go(p_pass(b, j, d))
            go(p_swap(b, j, d))

    def p_second_far(b, j):
        for d in (1, 3):
            p_pass(b, j, d).wait_recv()
        go(p_swap(b, j, 2))

    def p_done(b):
        for j in range(4):
            for d in range(4):
                p_swap(b, j, d).wait_recv()

    def z_dots(a, offsets, b, total=None):
        for s in offsets:
            m = (z + s) % NZ
            v = vp[b, m // 2, m % 2].reshape(WIDTH, WIDTH)
            term = jnp.dot(zb[a, s], v, preferred_element_type=F32)
            total = term if total is None else total + term
        return total

    def o_copy(d, h):
        m = 2 * ((x + d) % NX) + h
        slot = (m - z + NZ) % NZ
        return remote(
            zb.at[OCC, slot], ob.at[h, NX - d], os_.at[d - 1, h], or_.at[d - 1, h], at_x(d)
        )

    def o_arrived(slot):
        m = (z + slot) % NZ
        d, h = (m // 2 - x + NX) % NX, m % 2

        @pl.when(d == 0)
        def _():
            ob[h, 0] = zb[OCC, slot]

        @pl.when(d != 0)
        def _():
            remote(
                zb.at[OCC, slot], ob.at[h, NX - d], os_.at[d - 1, h], or_.at[d - 1, h], at_x(d)
            ).start()

    def o_done():
        for d in (1, 2, 3):
            for h in range(2):
                o_copy(d, h).wait_recv()

    rows = lax.broadcasted_iota(jnp.int32, (8, 128), 0)
    lanes = lax.broadcasted_iota(jnp.int32, (8, 128), 1)

    def place(p, q):
        return (rows == p) & (lanes == q)

    def y_copy(p, d):
        ref = hg.at[p, core, y]
        return remote(ref, ref, ys.at[p, d - 1], yr.at[p, d - 1], at_y(d))

    def y_swap(p, j):
        ref = hg.at[p, core, (y - j + NY) % NY]
        return remote(ref, ref, ks.at[p, j], kr.at[p, j], sibling)

    def y_start(p, value):
        hg[p, core, y] = value
        for d in (2, 1, 3):
            go(y_copy(p, d))
        go(y_swap(p, 0))

    def y_done(p):
        for d in (1, 3, 2):
            y_copy(p, d).wait_recv()
            go(y_swap(p, d))

    def x_copy(p, d):
        return remote(ps.at[p, d - 1], pr.at[p, d - 1], xs.at[p, d - 1], xr.at[p, d - 1], at_x(d))

    def b_copy(d):
        return remote(bl, bx.at[NX - d], bs.at[d - 1], br.at[d - 1], at_x(d))

    def b_start():
        for d in (2, 1, 3):
            go(b_copy(d))

    def b_done():
        for d in (1, 3, 2):
            b_copy(d).wait_recv()

    def x_start(p):
        for j in range(4):
            y_swap(p, j).wait_recv()
        h0 = hg[p, 0].reshape(WIDTH, WIDTH)
        h1 = hg[p, 1].reshape(WIDTH, WIDTH)
        for d in (2, 1, 3, 0):
            part = jnp.dot(ob[0, d], h0, preferred_element_type=F32)
            part += jnp.dot(ob[1, d], h1, preferred_element_type=F32)
            pf[p, d] = part
            if d:
                ps[p, d - 1] = part.astype(BF16)
                go(x_copy(p, d))

    def x_share(q):
        mine = jnp.zeros((8, 128), F32)
        for p in range(AUX):
            total = jnp.sum(bl[p].astype(F32) * pf[q, 0], axis=0)
            for d in (1, 2, 3):
                total += jnp.sum(bx[d, p].astype(F32) * pf[q, d], axis=0)
            mine = jnp.where(place(p, q), jnp.sum(total), mine)
        return mine

    def x_done(p):
        total = pf[p, 0]
        for d in (1, 3, 2):
            x_copy(p, d).wait_recv()
            total += pr[p, d - 1].astype(F32)
        return total

    def put(q):
        return pltpu.make_async_copy(dv.at[q], dressed.at[q], outs.at[q])

    def dot_all(left, right):
        return jnp.sum(left.astype(F32) * right.astype(F32))

    def out(q, total):
        value = total.astype(BF16)
        dv[q] = value
        put(q).start()

    def d_share(q, total):
        mine = jnp.zeros((8, 128), F32)
        for p in range(AUX):
            mine = jnp.where(place(p, q), dot_all(bl[p], total), mine)
        return mine

    def q_copies(stage):
        if stage == 0:
            buffer, mine, peers, base = qs, core, [sibling], 0
        elif stage == 1:
            buffer, mine, peers, base = qa, z, [at_z(i) for i in range(1, NZ)], 1
        else:
            buffer, mine, base = qb, x * NY + y, 8
            peers = [at_xy(i // NY, i % NY) for i in range(1, NX * NY)]
        ref = buffer.at[mine]
        return buffer, mine, [
            remote(ref, ref, qss.at[base + i], qsr.at[base + i], to) for i, to in enumerate(peers)
        ]

    def q_start(stage, value):
        buffer, mine, copies = q_copies(stage)
        buffer[mine] = value
        for copy in copies:
            go(copy)

    def q_done(stage):
        buffer, _, copies = q_copies(stage)
        for copy in copies:
            copy.wait_recv()
        return jnp.sum(buffer[...], axis=0)

    shares = []
    z_start(0)
    p_start(0)
    p_start(1)
    z_sub(0, 1, 0)
    z_sub(0, 1, 1)
    z_start(OCC)
    p_first(0)
    o_arrived(0)
    p_second(0, 0)
    z_sub(0, 2, 0)
    p_first(1)
    p_second(1, 0)
    z_sub(0, 2, 1)
    z_start(1)
    p_first_far(0)
    z_sub(OCC, 1, 0)
    p_second(0, 1)
    z_sub(OCC, 1, 1)
    o_arrived(7)
    o_arrived(1)
    p_first_far(1)
    z_sub(0, 3, 0)
    p_second(0, 3)
    z_sub(0, 3, 1)
    p_second_far(0, 0)
    z_sub(1, 1, 0)
    z_sub(1, 1, 1)
    p_second(1, 1)
    z_sub(OCC, 2, 0)
    z_sub(OCC, 2, 1)
    o_arrived(6)
    o_arrived(2)
    b_start()
    p_second(1, 3)
    z_last(0)
    z_start(2)
    p_second_far(1, 0)
    z_sub(1, 2, 0)
    z_sub(1, 2, 1)
    p_second(0, 2)
    z_sub(OCC, 3, 0)
    p_second_far(0, 1)
    z_sub(OCC, 3, 1)
    o_arrived(5)
    o_arrived(3)
    z_sub(2, 1, 0)
    p_second(1, 2)
    z_sub(2, 1, 1)
    p_second_far(0, 3)
    z_sub(1, 3, 0)
    p_second_far(1, 1)
    z_sub(1, 3, 1)
    p_second_far(1, 3)
    z_last(OCC)
    o_arrived(4)
    p_second_far(0, 2)
    z_sub(2, 2, 0)
    p_done(0)
    y_start(0, z_dots(0, range(NZ), VIRT).astype(BF16))
    z_sub(2, 2, 1)
    p_second_far(1, 2)
    z_last(1)
    y_start(1, z_dots(1, range(NZ), VIRT).astype(BF16))
    p_done(1)
    zb[3, 0] = z_dots(OCC, range(NZ), TENSOR).astype(BF16)
    z_start(3)
    z_sub(2, 3, 0)
    z_sub(2, 3, 1)
    z_sub(3, 1, 0)
    y_done(0)
    z_sub(3, 1, 1)
    z_last(2)
    y_start(2, z_dots(2, range(NZ), VIRT).astype(BF16))
    b_done()
    z_sub(3, 2, 0)
    z_sub(3, 2, 1)
    y_done(1)
    o_done()
    x_start(0)
    z_sub(3, 3, 0)
    x_start(1)
    z_sub(3, 3, 1)
    shares.append(x_share(0))
    y_done(2)
    shares.append(x_share(1))
    acc3 = z_dots(3, (0, 7, 1, 6, 2, 5, 3), VIRT)
    x_start(2)
    z_last(3)
    d3 = z_dots(3, (4,), VIRT, acc3)
    shares.append(d_share(3, d3))
    shares.append(x_share(2))
    q_start(0, shares[0] + shares[1] + shares[2] + shares[3])
    out(0, x_done(0))
    out(3, d3)
    q_start(1, q_done(0))
    out(1, x_done(1))
    q_start(2, q_done(1))
    out(2, x_done(2))
    polar[...] = q_done(2)
    for d in (1, 2, 3):
        for h in range(2):
            o_copy(d, h).wait_send()
    for copy in sent:
        copy.wait_send()
    for q in range(AUX):
        put(q).wait()


def on_device(tensor_tiles, tile_pairs, tile_counts, occupied, virtual):
    vmem = pl.BlockSpec(memory_space=pltpu.VMEM)
    hbm = pl.BlockSpec(memory_space=pl.ANY)
    dma = pltpu.SemaphoreType.DMA
    block = (TILE, WIDTH)
    shares, dressed = pl.pallas_call(
        kernel,
        out_shape=(
            jax.ShapeDtypeStruct((8, 128), F32),
            jax.ShapeDtypeStruct((AUX, *block), BF16),
        ),
        in_specs=[hbm] * 5,
        out_specs=(vmem, hbm),
        scratch_shapes=[
            pltpu.VMEM((4, AUX, TILE, TILE), BF16),
            pltpu.SMEM((4,), jnp.int32),
            pltpu.SMEM((1,), jnp.int32),
            pltpu.VMEM((AUX, *block), BF16),
            pltpu.VMEM((NX, AUX, *block), BF16),
            pltpu.VMEM((AUX + 1, NZ, *block), BF16),
            pltpu.VMEM((2, NX, 2, NY, *block), BF16),
            pltpu.VMEM((2, NX, *block), BF16),
            pltpu.VMEM((AUX, 2, NY, *block), BF16),
            pltpu.VMEM((AUX, 3, *block), BF16),
            pltpu.VMEM((AUX, 3, *block), BF16),
            pltpu.VMEM((AUX, NX, *block), F32),
            pltpu.VMEM((AUX, *block), BF16),
            pltpu.VMEM((2, 8, 128), F32),
            pltpu.VMEM((NZ, 8, 128), F32),
            pltpu.VMEM((NX * NY, 8, 128), F32),
            dma((5, 4, 2, PARTS)), dma((5, 4, 2, PARTS)),
            dma((2, 5, 2, 2)), dma((2, 5, 2, 2)),
            dma((2, 4, 4)), dma((2, 4, 4)),
            dma((3, 2)), dma((3, 2)),
            dma((3,)), dma((3,)),
            dma((4, 3)), dma((4, 3)),
            dma((4, 4)), dma((4, 4)),
            dma((4, 3)), dma((4, 3)),
            dma((23,)), dma((23,)), dma((5,)), dma((4,)),
        ],
        compiler_params=pltpu.CompilerParams(
            collective_id=0, has_side_effects=True, vmem_limit_bytes=56 * 2**20
        ),
        cost_estimate=pl.CostEstimate(flops=4 * 2**30, bytes_accessed=2**21, transcendentals=0),
    )(tensor_tiles, tile_pairs, tile_counts, occupied, virtual)
    return shares[:AUX, :AUX] / (NZ * WIDTH), dressed.transpose(1, 0, 2)


def solution(mesh):
    spread = P(("row", "col", "rep"))
    return jax.shard_map(
        on_device,
        mesh=mesh,
        in_specs=(
            P(("row", "col", "rep"), None, None, None),
            spread,
            spread,
            P(("col", "rep"), "row"),
            P(("col", "rep"), "row"),
        ),
        out_specs=(P(), P(("col", "rep"), None, "row")),
        check_vma=False,
    )
```

time: 109 us -> 93.9 us (0.86)
  Pallas kernels: 103 us -> 88.8 us
  local copies, waits for them, and re-layouts: 4.05 us -> 2.24 us
    pallas_call x1, Pallas kernels: 103 us -> 88.8 us  [on_device(): pl.pallas_call(kernel, out_shape=(jax.ShapeDtypeStruct((8, 128), F32), ja...]
    unnamed x9 -> x1, local copies, waits for them, and re-layouts: 4.05 us -> 2.24 us
where the time goes in v2:
time: 93.9 us; the launch traced here: 93.6 us
  Pallas kernels  88.8 us (95%)
  local copies, waits for them, and re-layouts  2.24 us (2%)
  between operations  1.28 us (1%)
  other arithmetic  1.25 us (1%)
    pallas_call x1, Pallas kernels, on_device(): pl.pallas_call(kernel, out_shape=(jax.ShapeDtypeStruct((8, 128), F32), ja...  88.8 us
    unnamed x1, local copies, waits for them, and re-layouts  2.24 us

profile of v2, /device:TPU:1, one launch (start us, length us, event | category | flops | bytes accessed | tf_op | source)
XLA Modules:
  0.0 93.6 jit_solution(11722239446364023934)
XLA Ops:
  1.3 88.8 %shard_map.68 = (f32[8,128]{1,0:T(8,128)}, bf16[4,128,512]{2,1,0:T(8,128)(2,1)}) custom-call(bf16[4,4,128,128]{3,2,1,0:T(8,128)(2,1)} %tiles_in.1, s32[4]{0:T(128)} %pairs_in.1, s32[1]{0:T(128)S(6)} %copy.8.counts_in, bf16[128,512]{1,0:T(8,128)(2,1)} %occ.1, bf16[128,512]{1,0:T(8,128)(2,1)} %virt.1), custom_call_target="tpu_custom_call" | custom-call | flops 4294967296 | bytes 2097152 | tf_op jit(solution)/shard_map/pallas_call | solution.py:431
  90.1 1.3 %slice_multiply_fusion = f32[4,4]{1,0:T(4,128)} fusion(f32[8,128]{1,0:T(8,128)} %get-tuple-element.4), kind=kLoop, calls=%fused_computation | loop fusion | flops 16 | bytes 128 | tf_op jit(solution)/shard_map/div | solution.py:471
  91.4 2.2 %copy.7 = bf16[128,4,512]{2,1,0:T(4,128)(2,1)} copy(bf16[128,4,512]{2,0,1:T(8,128)(2,1)} %bitcast.1) | data formatting | bytes 1048576

commit v3 on v2

--- a/solution.py
+++ b/solution.py
@@ -315,103 +315,103 @@
         return jnp.sum(buffer[...], axis=0)
 
     shares = []
+    z_start(1)
+    p_start(0)
     z_start(0)
-    p_start(0)
+    z_start(OCC)
     p_start(1)
+    p_second(0, 0)
+    z_sub(1, 1, 1)
+    z_start(2)
+    p_first(0)
+    p_first(1)
+    b_start()
+    p_second_far(0, 0)
+    z_sub(0, 1, 1)
+    z_sub(OCC, 1, 0)
+    z_sub(1, 2, 1)
+    z_sub(OCC, 1, 1)
+    p_second(1, 0)
+    z_sub(OCC, 2, 0)
+    p_first_far(0)
+    z_sub(2, 1, 1)
+    z_sub(OCC, 2, 1)
+    o_arrived(1)
+    z_sub(1, 1, 0)
+    p_second(0, 3)
+    z_sub(2, 1, 0)
     z_sub(0, 1, 0)
-    z_sub(0, 1, 1)
-    z_start(OCC)
-    p_first(0)
+    p_first_far(1)
+    z_sub(OCC, 3, 0)
+    z_sub(OCC, 3, 1)
+    p_second(0, 1)
+    z_sub(1, 2, 0)
+    p_second_far(0, 3)
+    o_arrived(3)
+    p_second(0, 2)
+    p_second_far(1, 0)
+    z_sub(0, 2, 1)
     o_arrived(0)
-    p_second(0, 0)
+    p_second(1, 1)
     z_sub(0, 2, 0)
-    p_first(1)
-    p_second(1, 0)
-    z_sub(0, 2, 1)
-    z_start(1)
-    p_first_far(0)
-    z_sub(OCC, 1, 0)
-    p_second(0, 1)
-    z_sub(OCC, 1, 1)
+    p_second(1, 2)
+    z_sub(1, 3, 0)
+    z_last(OCC)
+    z_sub(1, 3, 1)
+    p_second_far(0, 1)
+    p_second(1, 3)
+    o_arrived(4)
+    z_sub(2, 2, 1)
+    o_arrived(2)
+    p_second_far(0, 2)
+    p_done(0)
+    o_arrived(5)
+    p_second_far(1, 2)
     o_arrived(7)
-    o_arrived(1)
-    p_first_far(1)
+    z_sub(2, 2, 0)
     z_sub(0, 3, 0)
-    p_second(0, 3)
+    z_last(1)
+    p_second_far(1, 1)
+    y_start(1, z_dots(1, range(NZ), VIRT).astype(BF16))
     z_sub(0, 3, 1)
-    p_second_far(0, 0)
-    z_sub(1, 1, 0)
-    z_sub(1, 1, 1)
-    p_second(1, 1)
-    z_sub(OCC, 2, 0)
-    z_sub(OCC, 2, 1)
+    p_second_far(1, 3)
+    p_done(1)
+    z_sub(2, 3, 1)
+    z_sub(2, 3, 0)
     o_arrived(6)
-    o_arrived(2)
-    b_start()
-    p_second(1, 3)
-    z_last(0)
-    z_start(2)
-    p_second_far(1, 0)
-    z_sub(1, 2, 0)
-    z_sub(1, 2, 1)
-    p_second(0, 2)
-    z_sub(OCC, 3, 0)
-    p_second_far(0, 1)
-    z_sub(OCC, 3, 1)
-    o_arrived(5)
-    o_arrived(3)
-    z_sub(2, 1, 0)
-    p_second(1, 2)
-    z_sub(2, 1, 1)
-    p_second_far(0, 3)
-    z_sub(1, 3, 0)
-    p_second_far(1, 1)
-    z_sub(1, 3, 1)
-    p_second_far(1, 3)
-    z_last(OCC)
-    o_arrived(4)
-    p_second_far(0, 2)
-    z_sub(2, 2, 0)
-    p_done(0)
-    y_start(0, z_dots(0, range(NZ), VIRT).astype(BF16))
-    z_sub(2, 2, 1)
-    p_second_far(1, 2)
-    z_last(1)
-    y_start(1, z_dots(1, range(NZ), VIRT).astype(BF16))
-    p_done(1)
     zb[3, 0] = z_dots(OCC, range(NZ), TENSOR).astype(BF16)
     z_start(3)
-    z_sub(2, 3, 0)
-    z_sub(2, 3, 1)
+    z_last(0)
+    y_start(0, z_dots(0, range(NZ), VIRT).astype(BF16))
+    b_done()
+    o_done()
+    y_done(1)
+    z_last(2)
     z_sub(3, 1, 0)
+    y_start(2, z_dots(2, range(NZ), VIRT).astype(BF16))
+    z_sub(3, 1, 1)
+    x_start(1)
+    z_sub(3, 2, 0)
     y_done(0)
-    z_sub(3, 1, 1)
-    z_last(2)
-    y_start(2, z_dots(2, range(NZ), VIRT).astype(BF16))
-    b_done()
-    z_sub(3, 2, 0)
     z_sub(3, 2, 1)
-    y_done(1)
-    o_done()
     x_start(0)
+    shares.append(x_share(1))
     z_sub(3, 3, 0)
-    x_start(1)
     z_sub(3, 3, 1)
+    y_done(2)
+    acc3 = z_dots(3, (0, 7, 1, 6, 2, 5, 3), VIRT)
     shares.append(x_share(0))
-    y_done(2)
-    shares.append(x_share(1))
-    acc3 = z_dots(3, (0, 7, 1, 6, 2, 5, 3), VIRT)
     x_start(2)
+    shares.append(x_share(2))
     z_last(3)
     d3 = z_dots(3, (4,), VIRT, acc3)
     shares.append(d_share(3, d3))
-    shares.append(x_share(2))
     q_start(0, shares[0] + shares[1] + shares[2] + shares[3])
-    out(0, x_done(0))
-    out(3, d3)
     q_start(1, q_done(0))
     out(1, x_done(1))
+    out(3, d3)
     q_start(2, q_done(1))
+    out(0, x_done(0))
     out(2, x_done(2))
     polar[...] = q_done(2)
     for d in (1, 2, 3):

time: 93.9 us -> 90.7 us (0.966)
  Pallas kernels: 88.8 us -> 85.2 us
    pallas_call x1, Pallas kernels: 88.8 us -> 85.2 us  [on_device(): pl.pallas_call(kernel, out_shape=(jax.ShapeDtypeStruct((8, 128), F32), ja...]
where the time goes in v3:
time: 90.7 us; the launch traced here: 89.9 us
  Pallas kernels  85.2 us (94%)
  local copies, waits for them, and re-layouts  2.24 us (2%)
  between operations  1.28 us (1%)
  other arithmetic  1.25 us (1%)
    pallas_call x1, Pallas kernels, on_device(): pl.pallas_call(kernel, out_shape=(jax.ShapeDtypeStruct((8, 128), F32), ja...  85.2 us
    unnamed x1, local copies, waits for them, and re-layouts  2.24 us

profile of v3, /device:TPU:1, one launch (start us, length us, event | category | flops | bytes accessed | tf_op | source)
XLA Modules:
  0.0 89.9 jit_solution(6404014597856750121)
XLA Ops:
  1.3 85.2 %shard_map.68 = (f32[8,128]{1,0:T(8,128)}, bf16[4,128,512]{2,1,0:T(8,128)(2,1)}) custom-call(bf16[4,4,128,128]{3,2,1,0:T(8,128)(2,1)} %tiles_in.1, s32[4]{0:T(128)} %pairs_in.1, s32[1]{0:T(128)S(6)} %copy.8.counts_in, bf16[128,512]{1,0:T(8,128)(2,1)} %occ.1, bf16[128,512]{1,0:T(8,128)(2,1)} %virt.1), custom_call_target="tpu_custom_call" | custom-call | flops 4294967296 | bytes 2097152 | tf_op jit(solution)/shard_map/pallas_call | solution.py:431
  86.5 1.3 %slice_multiply_fusion = f32[4,4]{1,0:T(4,128)} fusion(f32[8,128]{1,0:T(8,128)} %get-tuple-element.4), kind=kLoop, calls=%fused_computation | loop fusion | flops 16 | bytes 128 | tf_op jit(solution)/shard_map/div | solution.py:471
  87.7 2.2 %copy.7 = bf16[128,4,512]{2,1,0:T(4,128)(2,1)} copy(bf16[128,4,512]{2,0,1:T(8,128)(2,1)} %bitcast.1) | data formatting | bytes 1048576

commit v4 on v3

--- a/solution.py
+++ b/solution.py
@@ -58,8 +58,7 @@
         load.start()
 
     barrier = pltpu.get_barrier_semaphore()
-    partners = [sibling] + [at_z(d) for d in range(1, NZ)]
-    partners += [at_xy(dx, dy) for dx in range(NX) for dy in range(NY) if dx or dy]
+    partners = [sibling, at_z(1), at_z(-1)] + [at_xy(d, 0) for d in (1, 2, 3)] + [at_xy(0, d) for d in (1, 2, 3)]
     for to in partners:
         pl.semaphore_signal(barrier, inc=1, device_id=to, device_id_type=MESH)
 
@@ -336,8 +335,8 @@
     p_first_far(0)
     z_sub(2, 1, 1)
     z_sub(OCC, 2, 1)
+    z_sub(1, 1, 0)
     o_arrived(1)
-    z_sub(1, 1, 0)
     p_second(0, 3)
     z_sub(2, 1, 0)
     z_sub(0, 1, 0)
@@ -362,12 +361,12 @@
     p_second(1, 3)
     o_arrived(4)
     z_sub(2, 2, 1)
-    o_arrived(2)
     p_second_far(0, 2)
     p_done(0)
+    o_arrived(2)
     o_arrived(5)
+    o_arrived(7)
     p_second_far(1, 2)
-    o_arrived(7)
     z_sub(2, 2, 0)
     z_sub(0, 3, 0)
     z_last(1)
@@ -408,12 +407,12 @@
     shares.append(d_share(3, d3))
     q_start(0, shares[0] + shares[1] + shares[2] + shares[3])
     q_start(1, q_done(0))
+    out(3, d3)
     out(1, x_done(1))
-    out(3, d3)
     q_start(2, q_done(1))
     out(0, x_done(0))
     out(2, x_done(2))
-    polar[...] = q_done(2)
+    polar[...] = q_done(2)[:AUX, :AUX] / (NZ * WIDTH)
     for d in (1, 2, 3):
         for h in range(2):
             o_copy(d, h).wait_send()
@@ -431,7 +430,7 @@
     shares, dressed = pl.pallas_call(
         kernel,
         out_shape=(
-            jax.ShapeDtypeStruct((8, 128), F32),
+            jax.ShapeDtypeStruct((AUX, AUX), F32),
             jax.ShapeDtypeStruct((AUX, *block), BF16),
         ),
         in_specs=[hbm] * 5,
@@ -468,7 +467,7 @@
         ),
         cost_estimate=pl.CostEstimate(flops=4 * 2**30, bytes_accessed=2**21, transcendentals=0),
     )(tensor_tiles, tile_pairs, tile_counts, occupied, virtual)
-    return shares[:AUX, :AUX] / (NZ * WIDTH), dressed.transpose(1, 0, 2)
+    return shares, dressed.transpose(1, 0, 2)
 
 
 def solution(mesh):

time: 90.7 us -> 88.3 us (0.974)
  other arithmetic: 1.25 us -> 0 us
  Pallas kernels: 85.2 us -> 84.1 us
    div x1 -> x0, other arithmetic: 1.25 us -> none  [on_device(): return (shares[:AUX, :AUX] / (NZ * WIDTH), dressed.transpose(1, 0, 2))]
    pallas_call x1, Pallas kernels: 85.2 us -> 84.1 us  [on_device(): pl.pallas_call(kernel, out_shape=(jax.ShapeDtypeStruct((AUX, AUX), F32),...]
    unnamed x1 -> x4, local copies, waits for them, and re-layouts: 2.24 us -> 2.82 us
where the time goes in v4:
time: 88.3 us; the launch traced here: 88.2 us
  Pallas kernels  84.1 us (95%)
  local copies, waits for them, and re-layouts  2.82 us (3%)
  between operations  1.29 us (1%)
    pallas_call x1, Pallas kernels, on_device(): pl.pallas_call(kernel, out_shape=(jax.ShapeDtypeStruct((AUX, AUX), F32),...  84.1 us
    unnamed x4, local copies, waits for them, and re-layouts  2.82 us

profile of v4, /device:TPU:1, one launch (start us, length us, event | category | flops | bytes accessed | tf_op | source)
XLA Modules:
  0.0 88.2 jit_solution(10110554906103652809)
XLA Ops:
  1.3 84.1 %shard_map.68 = (f32[4,4]{1,0:T(4,128)}, bf16[4,128,512]{2,1,0:T(8,128)(2,1)}) custom-call(bf16[4,4,128,128]{3,2,1,0:T(8,128)(2,1)} %tiles_in.1, s32[4]{0:T(128)} %pairs_in.1, s32[1]{0:T(128)S(6)} %copy.9.counts_in, bf16[128,512]{1,0:T(8,128)(2,1)} %occ.1, bf16[128,512]{1,0:T(8,128)(2,1)} %virt.1), custom_call_target="tpu_custom_call" | custom-call | flops 4294967296 | bytes 2097152 | tf_op jit(solution)/shard_map/pallas_call | solution.py:430
  85.4 0.0 copy-start
  85.4 2.2 %copy.7 = bf16[128,4,512]{2,1,0:T(4,128)(2,1)} copy(bf16[128,4,512]{2,0,1:T(8,128)(2,1)} %bitcast.1) | data formatting | bytes 1048576
  87.6 0.0 copy-done
  87.6 0.6 copy.10
Async XLA Ops:
  85.4 2.3 %copy-start = (f32[4,4]{1,0:T(4,128)S(1)}, f32[4,4]{1,0:T(4,128)}, u32[]{:S(2)}) copy-start(f32[4,4]{1,0:T(4,128)} %get-tuple-element.10) | copy-start | bytes 196

commit v5 on v4

--- a/solution.py
+++ b/solution.py
@@ -17,7 +17,7 @@
 
 def kernel(
     tiles_in, pairs_in, counts_in, occ, virt, polar, dressed,
-    tiles, pairs, counts, bl, bx, zb, vp, ob, hg, ps, pr, pf, dv, qs, qa, qb,
+    tiles, pairs, counts, bl, bx, zb, vp, ob, hg, ps, pr, pf, wide, dv, qs, qa, qb,
     zs, zr, vs, vr, us, ur, os_, or_, bs, br, ys, yr, ks, kr, xs, xr, qss, qsr, ins, outs,
 ):
     z, col, y = lax.axis_index("row"), lax.axis_index("col"), lax.axis_index("rep")
@@ -282,10 +282,13 @@
         dv[q] = value
         put(q).start()
 
-    def d_share(q, total):
+    def d_share(total):
+        return jnp.where(place(3, 3), dot_all(bl[3], total), 0.0)
+
+    def cross_share():
         mine = jnp.zeros((8, 128), F32)
-        for p in range(AUX):
-            mine = jnp.where(place(p, q), dot_all(bl[p], total), mine)
+        for p in range(AUX - 1):
+            mine = jnp.where(place(p, 3), dot_all(wide[3], wide[p]), mine)
         return mine
 
     def q_copies(stage):
@@ -305,13 +308,22 @@
         buffer, mine, copies = q_copies(stage)
         buffer[mine] = value
         for copy in copies:
-            go(copy)
+            copy.start() if stage == 2 else go(copy)
 
     def q_done(stage):
         buffer, _, copies = q_copies(stage)
         for copy in copies:
             copy.wait_recv()
         return jnp.sum(buffer[...], axis=0)
+
+    def drain():
+        for d in (1, 2, 3):
+            for h in range(2):
+                o_copy(d, h).wait_send()
+        for copy in sent:
+            copy.wait_send()
+        for q in range(AUX):
+            put(q).wait()
 
     shares = []
     z_start(1)
@@ -326,7 +338,6 @@
     p_first(1)
     b_start()
     p_second_far(0, 0)
-    z_sub(0, 1, 1)
     z_sub(OCC, 1, 0)
     z_sub(1, 2, 1)
     z_sub(OCC, 1, 1)
@@ -336,12 +347,13 @@
     z_sub(2, 1, 1)
     z_sub(OCC, 2, 1)
     z_sub(1, 1, 0)
+    z_sub(0, 1, 1)
+    p_second(0, 3)
+    z_sub(OCC, 3, 0)
+    z_sub(0, 1, 0)
     o_arrived(1)
-    p_second(0, 3)
     z_sub(2, 1, 0)
-    z_sub(0, 1, 0)
     p_first_far(1)
-    z_sub(OCC, 3, 0)
     z_sub(OCC, 3, 1)
     p_second(0, 1)
     z_sub(1, 2, 0)
@@ -353,14 +365,14 @@
     o_arrived(0)
     p_second(1, 1)
     z_sub(0, 2, 0)
+    z_last(OCC)
     p_second(1, 2)
     z_sub(1, 3, 0)
-    z_last(OCC)
     z_sub(1, 3, 1)
-    p_second_far(0, 1)
     p_second(1, 3)
     o_arrived(4)
     z_sub(2, 2, 1)
+    p_second_far(0, 1)
     p_second_far(0, 2)
     p_done(0)
     o_arrived(2)
@@ -371,23 +383,27 @@
     z_sub(0, 3, 0)
     z_last(1)
     p_second_far(1, 1)
-    y_start(1, z_dots(1, range(NZ), VIRT).astype(BF16))
+    wide[1] = z_dots(1, range(NZ), VIRT)
+    y_start(1, wide[1].astype(BF16))
     z_sub(0, 3, 1)
     p_second_far(1, 3)
     p_done(1)
     z_sub(2, 3, 1)
     z_sub(2, 3, 0)
     o_arrived(6)
-    zb[3, 0] = z_dots(OCC, range(NZ), TENSOR).astype(BF16)
+    wide[3] = z_dots(OCC, range(NZ), TENSOR)
+    zb[3, 0] = wide[3].astype(BF16)
     z_start(3)
     z_last(0)
-    y_start(0, z_dots(0, range(NZ), VIRT).astype(BF16))
     b_done()
+    wide[0] = z_dots(0, range(NZ), VIRT)
+    y_start(0, wide[0].astype(BF16))
+    z_last(2)
     o_done()
     y_done(1)
-    z_last(2)
     z_sub(3, 1, 0)
-    y_start(2, z_dots(2, range(NZ), VIRT).astype(BF16))
+    wide[2] = z_dots(2, range(NZ), VIRT)
+    y_start(2, wide[2].astype(BF16))
     z_sub(3, 1, 1)
     x_start(1)
     z_sub(3, 2, 0)
@@ -395,6 +411,7 @@
     z_sub(3, 2, 1)
     x_start(0)
     shares.append(x_share(1))
+    shares.append(cross_share())
     z_sub(3, 3, 0)
     z_sub(3, 3, 1)
     y_done(2)
@@ -404,22 +421,18 @@
     shares.append(x_share(2))
     z_last(3)
     d3 = z_dots(3, (4,), VIRT, acc3)
-    shares.append(d_share(3, d3))
-    q_start(0, shares[0] + shares[1] + shares[2] + shares[3])
+    shares.append(d_share(d3))
+    q_start(0, shares[0] + shares[1] + shares[2] + shares[3] + shares[4])
     q_start(1, q_done(0))
-    out(3, d3)
     out(1, x_done(1))
     q_start(2, q_done(1))
     out(0, x_done(0))
+    out(3, d3)
     out(2, x_done(2))
+    drain()
     polar[...] = q_done(2)[:AUX, :AUX] / (NZ * WIDTH)
-    for d in (1, 2, 3):
-        for h in range(2):
-            o_copy(d, h).wait_send()
-    for copy in sent:
+    for copy in q_copies(2)[2]:
         copy.wait_send()
-    for q in range(AUX):
-        put(q).wait()
 
 
 def on_device(tensor_tiles, tile_pairs, tile_counts, occupied, virtual):
@@ -448,6 +461,7 @@
             pltpu.VMEM((AUX, 3, *block), BF16),
             pltpu.VMEM((AUX, 3, *block), BF16),
             pltpu.VMEM((AUX, NX, *block), F32),
+            pltpu.VMEM((AUX, *block), F32),
             pltpu.VMEM((AUX, *block), BF16),
             pltpu.VMEM((2, 8, 128), F32),
             pltpu.VMEM((NZ, 8, 128), F32),

time: 88.3 us -> 88 us (level)
  no operation moved by 1% of the time
where the time goes in v5:
time: 88 us; the launch traced here: 87.9 us
  Pallas kernels  83.8 us (95%)
  local copies, waits for them, and re-layouts  2.82 us (3%)
  between operations  1.29 us (1%)
    pallas_call x1, Pallas kernels, on_device(): pl.pallas_call(kernel, out_shape=(jax.ShapeDtypeStruct((AUX, AUX), F32),...  83.8 us
    unnamed x4, local copies, waits for them, and re-layouts  2.82 us

profile of v5, /device:TPU:1, one launch (start us, length us, event | category | flops | bytes accessed | tf_op | source)
XLA Modules:
  0.0 87.9 jit_solution(7052764330846730903)
XLA Ops:
  1.3 83.8 %shard_map.68 = (f32[4,4]{1,0:T(4,128)}, bf16[4,128,512]{2,1,0:T(8,128)(2,1)}) custom-call(bf16[4,4,128,128]{3,2,1,0:T(8,128)(2,1)} %tiles_in.1, s32[4]{0:T(128)} %pairs_in.1, s32[1]{0:T(128)S(6)} %copy.9.counts_in, bf16[128,512]{1,0:T(8,128)(2,1)} %occ.1, bf16[128,512]{1,0:T(8,128)(2,1)} %virt.1), custom_call_target="tpu_custom_call" | custom-call | flops 4294967296 | bytes 2097152 | tf_op jit(solution)/shard_map/pallas_call | solution.py:443
  85.1 0.0 copy-start
  85.1 2.2 %copy.7 = bf16[128,4,512]{2,1,0:T(4,128)(2,1)} copy(bf16[128,4,512]{2,0,1:T(8,128)(2,1)} %bitcast.1) | data formatting | bytes 1048576
  87.3 0.0 copy-done
  87.3 0.6 copy.10
Async XLA Ops:
  85.1 2.3 %copy-start = (f32[4,4]{1,0:T(4,128)S(1)}, f32[4,4]{1,0:T(4,128)}, u32[]{:S(2)}) copy-start(f32[4,4]{1,0:T(4,128)} %get-tuple-element.10) | copy-start | bytes 196
